TPU v7x, 32 devices: a whole 2x2x4 slice. The times are simulated.
32 devices in a mesh: group: 2 (over x), lat: 16 (over z, y, core).
Axes of the slice: x: 2, y: 2, z: 4, core: 2. Of those that a mesh axis runs over, the one named last changes fastest.
Arguments:
- fields: bfloat16 [128, 40, 64, 128], P(('group', 'lat')), parts along dimension 0, may hold values from -6 to 6
- helm_coef: float32 [64, 5120], P('lat'), may hold values from 0.1 to 2
- weight_table: bfloat16 [64, 128, 128], replicated, may hold values from -0.1875 to 0.1875
- fetch_list: int32 [32, 7, 64], P(('group', 'lat')), parts along dimension 0, may hold values from 0 to 159, as said below
- source_owner: int32 [128, 40, 8], P(('group', 'lat')), parts along dimension 0, may hold values from 0 to 15, as said below
- source_slot: int32 [128, 40, 8], P(('group', 'lat')), parts along dimension 0, may hold values from 0 to 63
- weight_index: int32 [128, 40, 8], P(('group', 'lat')), parts along dimension 0, may hold values from 0 to 63
Outputs:
- adjusted: float32 [128, 4, 16, 5120], P(('group', 'lat')), parts along dimension 0
There are 2 independent parts, one for each index of `group`. A program takes and returns all parts, laid end to end along the dimension named above; an argument that names none is the same for every part. Nothing has to cross between parts.
Inputs may be any that keep to these rules, and one draw needn't show every extreme that they name: `fetch_list`: the 64 numbers of one list are distinct. `source_owner`: the band of a source differs from the band of its arrival row by at most 3.
All inputs are finite; a program needn't handle non-finite values.
Results may differ from a plain program's by a relative error of at most 0.0003.
Values may be sent and summed in bfloat16 or wider, within the bound.
A program may use at most 128 MiB of HBM per device.

v0:
```python
import jax
import jax.numpy as jnp
from jax import lax
from jax.sharding import PartitionSpec as P

FLD = 4
LEV = 16
SWEEPS = 2


lon_coupling = 0.25
lat_coupling = 1.0
lev_coupling = 0.25


def from_behind(value, axis, steps):
    count = lax.axis_size(axis)
    first, last = (max(0, -steps), min(count, count - steps))
    return lax.ppermute(value, axis, [(source, source + steps) for source in range(first, last)])


def extended_2(cells, sides, width):
    for axis, dim in sides:
        count = lax.axis_size(axis)
        ends = count - 1
        head = lax.slice_in_dim(cells, 0, width, axis=dim)
        tail = lax.slice_in_dim(cells, cells.shape[dim] - width, cells.shape[dim], axis=dim)
        cells = jnp.concatenate(
            [
                lax.ppermute(tail, axis, [(i, (i + 1) % count) for i in range(ends)]),
                cells,
                lax.ppermute(head, axis, [((i + 1) % count, i) for i in range(ends)]),
            ],
            axis=dim,
        )
    return cells


def couple(field, north_south):
    east_west = jnp.roll(field, 1, axis=3) + jnp.roll(field, -1, axis=3)
    padded = jnp.pad(field, ((0, 0), (0, 0), (1, 1), (0, 0)))
    vertical = padded[:, :, 2:] + padded[:, :, :-2]
    return lon_coupling * east_west + lat_coupling * north_south + lev_coupling * vertical


def per_device(
    fields, helm_coef, weight_table, fetch_list, source_owner, source_slot, weight_index
):
    rows = fields.shape[0]
    nblocks = fields.shape[1]
    planes = fields.shape[2]
    width = fields.shape[3]
    capacity = fetch_list.shape[2]
    reach = (fetch_list.shape[1] - 1) // 2
    position = lax.axis_index("lat")
    local_blocks = fields.reshape(rows * nblocks, planes, width)
    lists = fetch_list[0]
    pieces = []
    for step in range(2 * reach + 1):
        offset = step - reach
        if offset == 0:
            pieces.append(jnp.take(local_blocks, lists[step], axis=0))
        else:
            shard = from_behind(local_blocks, "lat", -offset)
            pieces.append(jnp.take(shard, lists[step], axis=0))
    gathered = jnp.concatenate(pieces, axis=0)
    pool_index = (source_owner - position + reach) * capacity + source_slot

    def one_row(inputs):
        row_ids, row_weights = inputs
        sources = jnp.take(gathered, row_ids, axis=0)
        weights = jnp.take(weight_table, row_weights, axis=0)
        return jnp.einsum("nrpy,nryx->pnx", sources, weights, preferred_element_type=jnp.float32)

    departed = lax.map(one_row, (pool_index, weight_index))
    departed = departed.reshape(rows, FLD, LEV, nblocks * width)
    total_coupling = 2.0 * (lon_coupling + lat_coupling + lev_coupling)
    diagonal = helm_coef[:, None, None, :] + total_coupling
    field = departed / diagonal
    for sweep in range(SWEEPS):
        extended = extended_2(field, (("lat", 0),), 1)
        field = (departed + couple(field, extended[2:] + extended[:-2])) / diagonal
    return field


def solution(mesh):
    return jax.shard_map(
        per_device,
        mesh=mesh,
        in_specs=(
            P(("group", "lat"), None, None, None),
            P("lat", None),
            P(),
            P(("group", "lat"), None, None),
            P(("group", "lat"), None, None),
            P(("group", "lat"), None, None),
            P(("group", "lat"), None, None),
        ),
        out_specs=P(("group", "lat"), None, None, None),
        check_vma=False,
    )
```

profile of v0, /device:TPU:14, one launch (start us, length us, event | category | flops | bytes accessed | tf_op | source)
XLA Modules:
  0.0 462.4 jit_solution(7657294925011889944)
XLA Ops:
  0.0 2.9 collective-permute-start
  2.9 3.4 collective-permute-start.1
  8.7 3.2 collective-permute-start.3
  11.9 3.3 collective-permute-start.4
  20.2 41.1 %collective-permute-done = bf16[160,64,128]{2,1,0:T(8,128)(2,1)} collective-permute-done((bf16[160,64,128]{2,1,0:T(8,128)(2,1)}, bf16[160,64,128]{2,1,0:T(8,128)(2,1)}, u32[]{:S(2)}, u32[]{:S(2)}) %collective-permute-start) | collective-permute-done | bytes 2621472 | tf_op jit(solution)/shard_map/ppermute | solution.py:19
  61.4 110.9 %collective-permute-start.5 = (bf16[160,64,128]{2,1,0:T(8,128)(2,1)}, bf16[160,64,128]{2,1,0:T(8,128)(2,1)}, u32[]{:S(2)}, u32[]{:S(2)}) collective-permute-start(bf16[160,64,128]{2,1,0:T(8,128)(2,1)} %bitcast.69), channel_id=1, source_target_pairs={{3,0},{4,1},{5,2},{6,3},{7,4},{8,5},{9,6},{10,7},{11,8},{12,9},{13... | collective-permute-start | bytes 7864328 | tf_op jit(solution)/shard_map/ppermute | solution.py:19
  175.7 51.0 %collective-permute-done.1 = bf16[160,64,128]{2,1,0:T(8,128)(2,1)} collective-permute-done((bf16[160,64,128]{2,1,0:T(8,128)(2,1)}, bf16[160,64,128]{2,1,0:T(8,128)(2,1)}, u32[]{:S(2)}, u32[]{:S(2)}) %collective-permute-start.1) | collective-permute-done | bytes 2621472 | tf_op jit(solution)/shard_map/ppermute | solution.py:19
  229.9 3.4 gather_fusion.4
  233.3 3.5 gather_fusion.6
  236.8 3.4 gather_fusion.7
  252.9 110.6 %while.10 = (s32[]{:T(128)}, f32[4,64,40,128]{3,2,1,0:T(8,128)}, s32[4,40,8]{1,2,0:T(8,128)}, bf16[64,128,128]{2,1,0:T(8,128)(2,1)S(1)}, s32[4,40,8]{2,1,0:T(8,1...) while((s32[]{:T(128)}, f32[4,64,40,128]{3,2,1,0:T(8,128)}, s32[4,40,8]{1,2,0:T(8,128)}, ...), condition=%wide.region_1.3_spmd, body=%wide.region_0.0_spmd.sunk | while | flops 678960768 | bytes 51151192 | solution.py:75
  253.8 10.7 %gather_fusion = bf16[320,128,128]{2,1,0:T(8,128)(2,1)} fusion(bf16[64,128,128]{2,1,0:T(8,128)(2,1)S(1)} %get-tuple-element.161, s32[1024]{0:T(1024)S(1)} %pad_clamp_fusion.11), kind=kCustom, calls=%fused_computation.1.clone.1 | custom fusion | bytes 20972800 | tf_op jit(solution)/shard_map/while/body/eval_jaxpr/jit(_take)/gather | solution.py:72
  264.6 6.8 %gather_fusion.1 = bf16[320,64,128]{2,1,0:T(8,128)(2,1)} fusion(bf16[448,64,128]{2,1,0:T(8,128)(2,1)} %get-tuple-element.163, s32[1024]{0:T(1024)S(1)} %pad_clamp_fusion.12), kind=kCustom, calls=%fused_computation.2.clone.1 | custom fusion | bytes 10487040 | tf_op jit(solution)/shard_map/while/body/eval_jaxpr/jit(_take)/gather | solution.py:71
  271.4 7.3 %fusion.40 = f32[1,64,40,128]{3,1,2,0:T(8,128)S(1)} fusion(bf16[40,8,128,128]{3,2,1,0:T(8,128)(2,1)} %bitcast.61, pred[40,8]{1,0:T(8,128)(4,1)S(1)} %get-tuple-element.142, bf16[40,8,64,128]{3,2,1,0:T(8,128)(2,1)} %bitcast.62, pred[40,8]{1,0:T(8,128)(4,1)S(1)} %get-tuple-element.143), kind=kOutput, calls=%fused_computation.16.clone.1 | convolution fusion | flops 678952960 | bytes 17040000 | tf_op jit(solution)/shard_map/while/body/eval_jaxpr/nrpy,nryx->pnx/dot_general | solution.py:73
  281.4 10.7 %gather_fusion = bf16[320,128,128]{2,1,0:T(8,128)(2,1)} fusion(bf16[64,128,128]{2,1,0:T(8,128)(2,1)S(1)} %get-tuple-element.161, s32[1024]{0:T(1024)S(1)} %pad_clamp_fusion.11), kind=kCustom, calls=%fused_computation.1.clone.1 | custom fusion | bytes 20972800 | tf_op jit(solution)/shard_map/while/body/eval_jaxpr/jit(_take)/gather | solution.py:72
  292.3 6.8 %gather_fusion.1 = bf16[320,64,128]{2,1,0:T(8,128)(2,1)} fusion(bf16[448,64,128]{2,1,0:T(8,128)(2,1)} %get-tuple-element.163, s32[1024]{0:T(1024)S(1)} %pad_clamp_fusion.12), kind=kCustom, calls=%fused_computation.2.clone.1 | custom fusion | bytes 10487040 | tf_op jit(solution)/shard_map/while/body/eval_jaxpr/jit(_take)/gather | solution.py:71
  299.0 7.3 %fusion.40 = f32[1,64,40,128]{3,1,2,0:T(8,128)S(1)} fusion(bf16[40,8,128,128]{3,2,1,0:T(8,128)(2,1)} %bitcast.61, pred[40,8]{1,0:T(8,128)(4,1)S(1)} %get-tuple-element.142, bf16[40,8,64,128]{3,2,1,0:T(8,128)(2,1)} %bitcast.62, pred[40,8]{1,0:T(8,128)(4,1)S(1)} %get-tuple-element.143), kind=kOutput, calls=%fused_computation.16.clone.1 | convolution fusion | flops 678952960 | bytes 17040000 | tf_op jit(solution)/shard_map/while/body/eval_jaxpr/nrpy,nryx->pnx/dot_general | solution.py:73
  309.1 10.7 %gather_fusion = bf16[320,128,128]{2,1,0:T(8,128)(2,1)} fusion(bf16[64,128,128]{2,1,0:T(8,128)(2,1)S(1)} %get-tuple-element.161, s32[1024]{0:T(1024)S(1)} %pad_clamp_fusion.11), kind=kCustom, calls=%fused_computation.1.clone.1 | custom fusion | bytes 20972800 | tf_op jit(solution)/shard_map/while/body/eval_jaxpr/jit(_take)/gather | solution.py:72
  319.9 6.8 %gather_fusion.1 = bf16[320,64,128]{2,1,0:T(8,128)(2,1)} fusion(bf16[448,64,128]{2,1,0:T(8,128)(2,1)} %get-tuple-element.163, s32[1024]{0:T(1024)S(1)} %pad_clamp_fusion.12), kind=kCustom, calls=%fused_computation.2.clone.1 | custom fusion | bytes 10487040 | tf_op jit(solution)/shard_map/while/body/eval_jaxpr/jit(_take)/gather | solution.py:71
  326.7 7.3 %fusion.40 = f32[1,64,40,128]{3,1,2,0:T(8,128)S(1)} fusion(bf16[40,8,128,128]{3,2,1,0:T(8,128)(2,1)} %bitcast.61, pred[40,8]{1,0:T(8,128)(4,1)S(1)} %get-tuple-element.142, bf16[40,8,64,128]{3,2,1,0:T(8,128)(2,1)} %bitcast.62, pred[40,8]{1,0:T(8,128)(4,1)S(1)} %get-tuple-element.143), kind=kOutput, calls=%fused_computation.16.clone.1 | convolution fusion | flops 678952960 | bytes 17040000 | tf_op jit(solution)/shard_map/while/body/eval_jaxpr/nrpy,nryx->pnx/dot_general | solution.py:73
  336.7 10.7 %gather_fusion = bf16[320,128,128]{2,1,0:T(8,128)(2,1)} fusion(bf16[64,128,128]{2,1,0:T(8,128)(2,1)S(1)} %get-tuple-element.161, s32[1024]{0:T(1024)S(1)} %pad_clamp_fusion.11), kind=kCustom, calls=%fused_computation.1.clone.1 | custom fusion | bytes 20972800 | tf_op jit(solution)/shard_map/while/body/eval_jaxpr/jit(_take)/gather | solution.py:72
  347.6 6.8 %gather_fusion.1 = bf16[320,64,128]{2,1,0:T(8,128)(2,1)} fusion(bf16[448,64,128]{2,1,0:T(8,128)(2,1)} %get-tuple-element.163, s32[1024]{0:T(1024)S(1)} %pad_clamp_fusion.12), kind=kCustom, calls=%fused_computation.2.clone.1 | custom fusion | bytes 10487040 | tf_op jit(solution)/shard_map/while/body/eval_jaxpr/jit(_take)/gather | solution.py:71
  354.3 7.3 %fusion.40 = f32[1,64,40,128]{3,1,2,0:T(8,128)S(1)} fusion(bf16[40,8,128,128]{3,2,1,0:T(8,128)(2,1)} %bitcast.61, pred[40,8]{1,0:T(8,128)(4,1)S(1)} %get-tuple-element.142, bf16[40,8,64,128]{3,2,1,0:T(8,128)(2,1)} %bitcast.62, pred[40,8]{1,0:T(8,128)(4,1)S(1)} %get-tuple-element.143), kind=kOutput, calls=%fused_computation.16.clone.1 | convolution fusion | flops 678952960 | bytes 17040000 | tf_op jit(solution)/shard_map/while/body/eval_jaxpr/nrpy,nryx->pnx/dot_general | solution.py:73
  363.5 6.4 %reshape.96 = f32[4,4,16,5120]{3,2,1,0:T(8,128)} reshape(f32[4,64,40,128]{3,2,1,0:T(8,128)} %get-tuple-element.38) | data formatting | bytes 10485760 | tf_op jit(solution)/shard_map/reshape | solution.py:76
  369.9 3.0 broadcast_divide_fusion
  377.8 5.8 %fusion.32 = (f32[4,4,16,5119]{3,2,1,0:T(8,128)}, f32[4,4,16,5119]{3,2,1,0:T(8,128)}) fusion(f32[4,4,16,5120]{3,2,1,0:T(8,128)S(1)} %broadcast_divide_fusion), kind=kLoop, calls=%fused_computation.88 | loop fusion | bytes 20967424 | tf_op jit(solution)/shard_map/jit(_roll_static)/slice | solution.py:40
  383.6 20.7 %collective-permute-done.6 = f32[1,4,16,5120]{3,2,1,0:T(8,128)S(1)} collective-permute-done((f32[1,4,16,5120]{3,2,1,0:T(8,128)S(1)}, f32[1,4,16,5120]{3,2,1,0:T(8,128)S(1)}, u32[]{:S(2)}, u32[]{:S(2)}) %collective-permute-start.6) | collective-permute-done | bytes 1310752 | tf_op jit(solution)/shard_map/ppermute | solution.py:32
  405.8 13.8 %fusion.17 = f32[4,4,16,5120]{3,2,1,0:T(8,128)S(1)} fusion(f32[4,4,16,5120]{3,2,1,0:T(8,128)} %reshape.96, f32[4,4,16,5120]{3,2,1,0:T(8,128)} %copy-done.1, f32[1,4,16,5120]{3,2,1,0:T(8,128)} %copy-done.5, f32[1,4,16,5120]{3,2,1,0:T(8,128)} %copy-done.4, f32[4,4,16,5119]{3,2,1,0:T(8,128)} %get-tuple-element.86, f32[4,4,16,1]{3,2,1,0:T(8,128)S(1)} %get-tuple-element.88, ...), kind=kLoop, calls=%fused_computation.36 | loop fusion | flops 17039360 | bytes 28917760 | tf_op jit(solution)/shard_map/div | solution.py:82
  419.9 3.8 collective-permute-start.8
  425.7 6.1 %fusion.29 = (f32[4,4,16,5119]{3,2,1,0:T(8,128)}, f32[4,4,16,5119]{3,2,1,0:T(8,128)}) fusion(f32[4,4,16,5120]{3,2,1,0:T(8,128)S(1)} %fusion.17), kind=kLoop, calls=%fused_computation.85 | loop fusion | bytes 20967424 | tf_op jit(solution)/shard_map/jit(_roll_static)/slice | solution.py:40
  431.8 20.7 %collective-permute-done.8 = f32[1,4,16,5120]{3,2,1,0:T(8,128)} collective-permute-done((f32[1,4,16,5120]{3,2,1,0:T(8,128)S(1)}, f32[1,4,16,5120]{3,2,1,0:T(8,128)}, u32[]{:S(2)}, u32[]{:S(2)}) %collective-permute-start.8) | collective-permute-done | bytes 1310752 | tf_op jit(solution)/shard_map/ppermute | solution.py:32
  452.5 9.9 %fusion.22 = f32[4,4,16,5120]{3,2,1,0:T(8,128)} fusion(f32[4,4,16,5120]{3,2,1,0:T(8,128)} %reshape.96, f32[4,4,16,5120]{3,2,1,0:T(8,128)S(1)} %fusion.17, f32[1,4,16,5120]{3,2,1,0:T(8,128)} %collective-permute-done.9, f32[1,4,16,5120]{3,2,1,0:T(8,128)} %collective-permute-done.8, f32[4,4,16,5119]{3,2,1,0:T(8,128)} %get-tuple-element.80, ...), kind=kLoop, calls=%fused_computation.41 | loop fusion | flops 17039360 | bytes 28917760 | tf_op jit(solution)/shard_map/div | solution.py:82
  (90 shorter events, 46.4 us)
Async XLA Ops:
  0.0 61.4 %collective-permute-start = (bf16[160,64,128]{2,1,0:T(8,128)(2,1)}, bf16[160,64,128]{2,1,0:T(8,128)(2,1)}, u32[]{:S(2)}, u32[]{:S(2)}) collective-permute-start(bf16[160,64,128]{2,1,0:T(8,128)(2,1)} %bitcast.63), channel_id=1, source_target_pairs={{0,3},{1,4},{2,5},{3,6},{4,7},{5,8},{6,9},{7,10},{8,11},{9,12},{10... | collective-permute-start | bytes 7864328 | tf_op jit(solution)/shard_map/ppermute | solution.py:19
  2.9 223.8 %collective-permute-start.1 = (bf16[160,64,128]{2,1,0:T(8,128)(2,1)}, bf16[160,64,128]{2,1,0:T(8,128)(2,1)}, u32[]{:S(2)}, u32[]{:S(2)}) collective-permute-start(bf16[160,64,128]{2,1,0:T(8,128)(2,1)} %bitcast.64), channel_id=1, source_target_pairs={{0,2},{1,3},{2,4},{3,5},{4,6},{5,7},{6,8},{7,9},{8,10},{9,11},{10,... | collective-permute-start | bytes 7864328 | tf_op jit(solution)/shard_map/ppermute | solution.py:19
  6.3 223.6 %collective-permute-start.2 = (bf16[160,64,128]{2,1,0:T(8,128)(2,1)}, bf16[160,64,128]{2,1,0:T(8,128)(2,1)}, u32[]{:S(2)}, u32[]{:S(2)}) collective-permute-start(bf16[160,64,128]{2,1,0:T(8,128)(2,1)} %bitcast.65), channel_id=1, source_target_pairs={{0,1},{1,2},{2,3},{3,4},{4,5},{5,6},{6,7},{7,8},{8,9},{9,10},{10,1... | collective-permute-start | bytes 7864328 | tf_op jit(solution)/shard_map/ppermute | solution.py:19
  8.7 224.6 %collective-permute-start.3 = (bf16[160,64,128]{2,1,0:T(8,128)(2,1)}, bf16[160,64,128]{2,1,0:T(8,128)(2,1)}, u32[]{:S(2)}, u32[]{:S(2)}) collective-permute-start(bf16[160,64,128]{2,1,0:T(8,128)(2,1)} %bitcast.66), channel_id=1, source_target_pairs={{1,0},{2,1},{3,2},{4,3},{5,4},{6,5},{7,6},{8,7},{9,8},{10,9},{11,1... | collective-permute-start | bytes 7864328 | tf_op jit(solution)/shard_map/ppermute | solution.py:19
  11.9 224.9 %collective-permute-start.4 = (bf16[160,64,128]{2,1,0:T(8,128)(2,1)}, bf16[160,64,128]{2,1,0:T(8,128)(2,1)}, u32[]{:S(2)}, u32[]{:S(2)}) collective-permute-start(bf16[160,64,128]{2,1,0:T(8,128)(2,1)} %bitcast.67), channel_id=1, source_target_pairs={{2,0},{3,1},{4,2},{5,3},{6,4},{7,5},{8,6},{9,7},{10,8},{11,9},{12,... | collective-permute-start | bytes 7864328 | tf_op jit(solution)/shard_map/ppermute | solution.py:19
  61.4 187.7 %collective-permute-start.5 = (bf16[160,64,128]{2,1,0:T(8,128)(2,1)}, bf16[160,64,128]{2,1,0:T(8,128)(2,1)}, u32[]{:S(2)}, u32[]{:S(2)}) collective-permute-start(bf16[160,64,128]{2,1,0:T(8,128)(2,1)} %bitcast.69), channel_id=1, source_target_pairs={{3,0},{4,1},{5,2},{6,3},{7,4},{8,5},{9,6},{10,7},{11,8},{12,9},{13... | collective-permute-start | bytes 7864328 | tf_op jit(solution)/shard_map/ppermute | solution.py:19
  240.2 6.4 %copy-start.2 = (bf16[64,64,128]{2,1,0:T(8,128)(2,1)S(1)}, bf16[64,64,128]{2,1,0:T(8,128)(2,1)}, u32[]{:S(2)}) copy-start(bf16[64,64,128]{2,1,0:T(8,128)(2,1)} %gather_fusion.6) | copy-start | bytes 3145732
  240.2 7.7 %copy-start.3 = (bf16[64,64,128]{2,1,0:T(8,128)(2,1)S(1)}, bf16[64,64,128]{2,1,0:T(8,128)(2,1)}, u32[]{:S(2)}) copy-start(bf16[64,64,128]{2,1,0:T(8,128)(2,1)} %gather_fusion.7) | copy-start | bytes 3145732
  245.3 7.6 %copy-start = (bf16[64,128,128]{2,1,0:T(8,128)(2,1)S(1)}, bf16[64,128,128]{2,1,0:T(8,128)(2,1)}, u32[]{:S(2)}) copy-start(bf16[64,128,128]{2,1,0:T(8,128)(2,1)} %param.13) | copy-start | bytes 6291460
  372.9 10.7 %copy-start.1 = (f32[4,4,16,5120]{3,2,1,0:T(8,128)}, f32[4,4,16,5120]{3,2,1,0:T(8,128)S(1)}, u32[]{:S(2)}) copy-start(f32[4,4,16,5120]{3,2,1,0:T(8,128)S(1)} %broadcast_divide_fusion) | copy-start | bytes 15728644
  373.3 31.1 %collective-permute-start.6 = (f32[1,4,16,5120]{3,2,1,0:T(8,128)S(1)}, f32[1,4,16,5120]{3,2,1,0:T(8,128)S(1)}, u32[]{:S(2)}, u32[]{:S(2)}) collective-permute-start(f32[1,4,16,5120]{3,2,1,0:T(8,128)S(1)} %get-tuple-element.89), channel_id=1, source_target_pairs={{1,0},{2,1},{3,2},{4,3},{5,4},{6,5},{7,6},{8,7},{9,8},{10,9},{11,1... | collective-permute-start | bytes 3932168 | tf_op jit(solution)/shard_map/ppermute | solution.py:32
  375.2 29.4 %collective-permute-start.7 = (f32[1,4,16,5120]{3,2,1,0:T(8,128)S(1)}, f32[1,4,16,5120]{3,2,1,0:T(8,128)S(1)}, u32[]{:S(2)}, u32[]{:S(2)}) collective-permute-start(f32[1,4,16,5120]{3,2,1,0:T(8,128)S(1)} %get-tuple-element.90), channel_id=1, source_target_pairs={{0,1},{1,2},{2,3},{3,4},{4,5},{5,6},{6,7},{7,8},{8,9},{9,10},{10,1... | collective-permute-start | bytes 3932168 | tf_op jit(solution)/shard_map/ppermute | solution.py:30
  404.3 1.1 copy-start.4
  404.6 1.2 copy-start.5
  419.9 32.5 %collective-permute-start.8 = (f32[1,4,16,5120]{3,2,1,0:T(8,128)S(1)}, f32[1,4,16,5120]{3,2,1,0:T(8,128)}, u32[]{:S(2)}, u32[]{:S(2)}) collective-permute-start(f32[1,4,16,5120]{3,2,1,0:T(8,128)S(1)} %get-tuple-element.83), channel_id=1, source_target_pairs={{1,0},{2,1},{3,2},{4,3},{5,4},{6,5},{7,6},{8,7},{9,8},{10,9},{11,1... | collective-permute-start | bytes 3932168 | tf_op jit(solution)/shard_map/ppermute | solution.py:32
  423.8 28.7 %collective-permute-start.9 = (f32[1,4,16,5120]{3,2,1,0:T(8,128)S(1)}, f32[1,4,16,5120]{3,2,1,0:T(8,128)}, u32[]{:S(2)}, u32[]{:S(2)}) collective-permute-start(f32[1,4,16,5120]{3,2,1,0:T(8,128)S(1)} %get-tuple-element.84), channel_id=1, source_target_pairs={{0,1},{1,2},{2,3},{3,4},{4,5},{5,6},{6,7},{7,8},{8,9},{9,10},{10,1... | collective-permute-start | bytes 3932168 | tf_op jit(solution)/shard_map/ppermute | solution.py:30
where the time goes:
time: 466 us; the launch traced here: 462 us
  starting transfers between devices  136 us (29%)
  waiting for transfers between devices  135 us (29%)
  local copies, waits for them, and re-layouts  123 us (26%)
  other arithmetic  38.9 us (8%)
  matrix products  29.2 us (6%)
    ppermute x6, starting transfers between devices, from_behind(): lax.ppermute(value, axis, [(source, source + steps) for source in range(f...  126 us
    ppermute x6, waiting for transfers between devices, from_behind(): lax.ppermute(value, axis, [(source, source + steps) for source in range(f...  92.9 us
    gather x4, local copies, waits for them, and re-layouts, one_row(): weights = jnp.take(weight_table, row_weights, axis=0)  42.9 us
    ppermute x2, waiting for transfers between devices, extended_2(): lax.ppermute(head, axis, [((i + 1) % count, i) for i in range(ends)])  41.4 us
    dot_general x4, matrix products, one_row(): jnp.einsum('nrpy,nryx->pnx', sources, weights, preferred_element_type=jnp...  29.2 us
    gather x4, local copies, waits for them, and re-layouts, one_row(): sources = jnp.take(gathered, row_ids, axis=0)  27.1 us
    div x2, other arithmetic, per_device(): field = (departed + couple(field, extended[2:] + extended[:-2])) / diagonal  23.7 us
    gather x6, local copies, waits for them, and re-layouts, per_device(): pieces.append(jnp.take(shard, lists[step], axis=0))  17.7 us
  transfers between devices with their start and end apart: 10, of which 6 were waited for; matrix products, arithmetic and copies ran while one was open for 9% of the time, Pallas kernels for 0%

commit v1 on v0

v1 whole, which is shorter than its diff:
```python
import functools

import jax
import jax.numpy as jnp
from jax import lax
from jax.experimental import pallas as pl
from jax.experimental.pallas import tpu as pltpu
from jax.sharding import PartitionSpec as P

FLD = 4
LEV = 16
SWEEPS = 2

lon_coupling = 0.25
lat_coupling = 1.0
lev_coupling = 0.25

MESH = pl.DeviceIdType.MESH


def relax_kernel(
    reach,
    bands,
    fields_ref,
    lists_smem,
    lists_vmem,
    helm_ref,
    table_hbm,
    pool_index_hbm,
    weight_index_hbm,
    out_hbm,
    table,
    pool_index,
    weight_index,
    asked_vmem,
    asked,
    packed,
    pool,
    inverse,
    departed,
    first,
    second,
    local_sem,
    list_send,
    list_recv,
    asked_sem,
    block_send,
    block_recv,
    halo_send,
    halo_recv,
    out_sem,
):
    me = lax.axis_index("lat")
    offsets, cap = lists_smem.shape
    rows, planes, lon = departed.shape
    width = fields_ref.shape[2]
    nblocks = lon // width
    taps = pool_index.shape[2]
    others = [r for r in range(offsets) if r != reach]
    others.sort(key=lambda r: -abs(r - reach))

    def there(step):
        band = me + (step - reach)
        return (band >= 0) & (band < bands)

    barrier = pltpu.get_barrier_semaphore()
    count = jnp.int32(0)
    for r in others:

        @pl.when(there(r))
        def _():
            pl.semaphore_signal(barrier, inc=1, device_id={"lat": me + (r - reach)}, device_id_type=MESH)

        count = count + there(r).astype(jnp.int32)
    pl.semaphore_wait(barrier, count)

    def list_copy(r):
        back = 2 * reach - r
        return pltpu.make_async_remote_copy(
            src_ref=lists_vmem,
            dst_ref=asked_vmem.at[back],
            send_sem=list_send.at[r],
            recv_sem=list_recv.at[back],
            device_id={"lat": me + (r - reach)},
            device_id_type=MESH,
        )

    for r in others:

        @pl.when(there(r))
        def _():
            list_copy(r).start()

    locals_ = [
        pltpu.make_async_copy(table_hbm, table, local_sem.at[0]),
        pltpu.make_async_copy(pool_index_hbm, pool_index, local_sem.at[1]),
        pltpu.make_async_copy(weight_index_hbm, weight_index, local_sem.at[2]),
    ]
    for copy in locals_:
        copy.start()

    def asked_copy(r):
        return pltpu.make_async_copy(asked_vmem.at[r], asked.at[r], asked_sem.at[r])

    for r in others:

        @pl.when(there(r))
        def _():
            list_copy(2 * reach - r).wait_recv()
            asked_copy(r).start()

    def block_copy(r):
        back = 2 * reach - r
        return pltpu.make_async_remote_copy(
            src_ref=packed.at[r],
            dst_ref=pool.at[pl.ds(back * cap, cap)],
            send_sem=block_send.at[r],
            recv_sem=block_recv.at[back],
            device_id={"lat": me + (r - reach)},
            device_id_type=MESH,
        )

    unroll = 8 if cap % 8 == 0 else 1
    for r in others:

        @pl.when(there(r))
        def _():
            asked_copy(r).wait()

            def pack(j, carry):
                for u in range(unroll):
                    packed[r, j * unroll + u] = fields_ref[asked[r, 2 * reach - r, j * unroll + u]]
                return carry

            lax.fori_loop(0, cap // unroll, pack, 0)
            block_copy(r).start()

    def pack_own(j, carry):
        for u in range(unroll):
            pool[reach * cap + j * unroll + u] = fields_ref[lists_smem[reach, j * unroll + u]]
        return carry

    lax.fori_loop(0, cap // unroll, pack_own, 0)

    total_coupling = 2.0 * (lon_coupling + lat_coupling + lev_coupling)
    inverse[...] = 1.0 / (helm_ref[...] + total_coupling)

    @pl.when(me == 0)
    def _():
        first[0] = jnp.zeros((planes, lon), jnp.float32)
        second[0] = jnp.zeros((planes, lon), jnp.float32)

    @pl.when(me == bands - 1)
    def _():
        first[rows + 1] = jnp.zeros((planes, lon), jnp.float32)
        second[rows + 1] = jnp.zeros((planes, lon), jnp.float32)

    for copy in locals_:
        copy.wait()
    for r in others:

        @pl.when(there(r))
        def _():
            block_copy(2 * reach - r).wait_recv()

    north, south = me > 0, me < bands - 1

    def halo_copy(sweep, way, f):
        held = (first, second)[sweep]
        planes_f = pl.ds(pl.multiple_of(f * LEV, LEV), LEV)
        return pltpu.make_async_remote_copy(
            src_ref=held.at[1 if way == 0 else rows, planes_f],
            dst_ref=held.at[rows + 1 if way == 0 else 0, planes_f],
            send_sem=halo_send.at[sweep, way, f],
            recv_sem=halo_recv.at[sweep, way, f],
            device_id={"lat": me - 1 if way == 0 else me + 1},
            device_id_type=MESH,
        )

    def interpolate(row):
        def one_block(b, carry):
            columns = pl.ds(pl.multiple_of(b * width, width), width)
            sources = jnp.concatenate([pool[pool_index[row, b, t]] for t in range(taps)], axis=1)
            weights = jnp.concatenate([table[weight_index[row, b, t]] for t in range(taps)], axis=0)
            value = jnp.dot(sources, weights, preferred_element_type=jnp.float32)
            departed[row, :, columns] = value
            first[row + 1, :, columns] = value * inverse[row : row + 1, columns]
            return carry

        lax.fori_loop(0, nblocks, one_block, 0)

    order = [0, rows - 1] + list(range(1, rows - 1))
    for row in order:
        interpolate(row)
        if row == 0:

            @pl.when(north)
            def _():
                for f in range(FLD):
                    halo_copy(0, 0, f).start()

        if row == rows - 1:

            @pl.when(south)
            def _():
                for f in range(FLD):
                    halo_copy(0, 1, f).start()

    chunk = 1024 if lon % 1024 == 0 else width
    lane = 128

    def relax(held, result, row, f):
        planes_f = pl.ds(pl.multiple_of(f * LEV, LEV), LEV)
        for start in range(0, lon, chunk):
            here = pl.ds(start, chunk)
            mid = held[row + 1, planes_f, here]
            west = held[row + 1, planes_f, pl.ds((start - lane) % lon, lane)]
            east = held[row + 1, planes_f, pl.ds((start + chunk) % lon, lane)]
            wide = jnp.concatenate([west, mid, east], axis=1)
            span = chunk + 2 * lane
            beside = pltpu.roll(wide, 1, 1) + pltpu.roll(wide, span - 1, 1)
            beside = beside[:, lane : lane + chunk]
            level = lax.broadcasted_iota(jnp.int32, (LEV, chunk), 0)
            above = jnp.where(level > 0, pltpu.roll(mid, 1, 0), 0.0)
            below = jnp.where(level < LEV - 1, pltpu.roll(mid, LEV - 1, 0), 0.0)
            across = held[row, planes_f, here] + held[row + 2, planes_f, here]
            coupled = lon_coupling * beside + lat_coupling * across + lev_coupling * (above + below)
            value = (departed[row, planes_f, here] + coupled) * inverse[row : row + 1, here]
            if result is departed:
                result[row, planes_f, here] = value
            else:
                result[row + 1, planes_f, here] = value

    def out_copy(row, f):
        planes_f = pl.ds(pl.multiple_of(f * LEV, LEV), LEV)
        return pltpu.make_async_copy(departed.at[row, planes_f], out_hbm.at[row, planes_f], out_sem.at[row, f])

    inner, edges = list(range(1, rows - 1)), [0, rows - 1]

    def arrived(sweep, f):
        @pl.when(north)
        def _():
            halo_copy(sweep, 1, f).wait_recv()

        @pl.when(south)
        def _():
            halo_copy(sweep, 0, f).wait_recv()

    def first_inner(f, carry):
        for row in inner:
            relax(first, second, row, f)
        return carry

    lax.fori_loop(0, FLD, first_inner, 0)

    def first_edges(f, carry):
        arrived(0, f)
        relax(first, second, 0, f)

        @pl.when(north)
        def _():
            halo_copy(1, 0, f).start()

        relax(first, second, rows - 1, f)

        @pl.when(south)
        def _():
            halo_copy(1, 1, f).start()

        return carry

    lax.fori_loop(0, FLD, first_edges, 0)

    def second_inner(f, carry):
        for row in inner:
            relax(second, departed, row, f)
            out_copy(row, f).start()
        return carry

    lax.fori_loop(0, FLD, second_inner, 0)

    def second_edges(f, carry):
        arrived(1, f)
        for row in edges:
            relax(second, departed, row, f)
            out_copy(row, f).start()
        return carry

    lax.fori_loop(0, FLD, second_edges, 0)

    for r in others:

        @pl.when(there(r))
        def _():
            list_copy(r).wait_send()
            block_copy(r).wait_send()

    def finish(f, carry):
        for sweep in range(SWEEPS):

            @pl.when(north)
            def _():
                halo_copy(sweep, 0, f).wait_send()

            @pl.when(south)
            def _():
                halo_copy(sweep, 1, f).wait_send()

        for row in range(rows):
            out_copy(row, f).wait()
        return carry

    lax.fori_loop(0, FLD, finish, 0)


def per_device(bands, fields, helm_coef, weight_table, fetch_list, source_owner, source_slot, weight_index):
    rows, nblocks, planes, width = fields.shape
    offsets, cap = fetch_list.shape[1:]
    reach = (offsets - 1) // 2
    lon = nblocks * width
    position = lax.axis_index("lat")
    lists = fetch_list[0]
    pool_index = (source_owner - position + reach) * cap + source_slot
    vmem = pl.BlockSpec(memory_space=pltpu.VMEM)
    smem = pl.BlockSpec(memory_space=pltpu.SMEM)
    anywhere = pl.BlockSpec(memory_space=pl.ANY)
    dma = pltpu.SemaphoreType.DMA
    result = pl.pallas_call(
        functools.partial(relax_kernel, reach, bands),
        out_shape=jax.ShapeDtypeStruct((rows, planes, lon), jnp.float32),
        in_specs=[vmem, smem, vmem, vmem, anywhere, anywhere, anywhere],
        out_specs=anywhere,
        scratch_shapes=[
            pltpu.VMEM(weight_table.shape, weight_table.dtype),
            pltpu.SMEM(pool_index.shape, jnp.int32),
            pltpu.SMEM(weight_index.shape, jnp.int32),
            pltpu.VMEM((offsets, offsets, cap), jnp.int32),
            pltpu.SMEM((offsets, offsets, cap), jnp.int32),
            pltpu.VMEM((offsets, cap, planes, width), fields.dtype),
            pltpu.VMEM((offsets * cap, planes, width), fields.dtype),
            pltpu.VMEM((rows, lon), jnp.float32),
            pltpu.VMEM((rows, planes, lon), jnp.float32),
            pltpu.VMEM((rows + 2, planes, lon), jnp.float32),
            pltpu.VMEM((rows + 2, planes, lon), jnp.float32),
            dma((3,)),
            dma((offsets,)),
            dma((offsets,)),
            dma((offsets,)),
            dma((offsets,)),
            dma((offsets,)),
            dma((SWEEPS, 2, FLD)),
            dma((SWEEPS, 2, FLD)),
            dma((rows, FLD)),
        ],
        compiler_params=pltpu.CompilerParams(
            collective_id=0, has_side_effects=True, vmem_limit_bytes=56 * 1024 * 1024
        ),
        cost_estimate=pl.CostEstimate(
            flops=2 * source_owner.size * planes * width * width,
            bytes_accessed=fields.size * 2 + weight_table.size * 2 + rows * planes * lon * 4,
            transcendentals=0,
        ),
    )(fields.reshape(rows * nblocks, planes, width), lists, lists, helm_coef, weight_table, pool_index, weight_index)
    return result.reshape(rows, FLD, LEV, lon)


def solution(mesh):
    return jax.shard_map(
        functools.partial(per_device, mesh.shape["lat"]),
        mesh=mesh,
        in_specs=(
            P(("group", "lat"), None, None, None),
            P("lat", None),
            P(),
            P(("group", "lat"), None, None),
            P(("group", "lat"), None, None),
            P(("group", "lat"), None, None),
            P(("group", "lat"), None, None),
        ),
        out_specs=P(("group", "lat"), None, None, None),
        check_vma=False,
    )
```

time: 466 us -> 180 us (0.39)
  Pallas kernels: 0 us -> 169 us
  starting transfers between devices: 136 us -> 0 us
  waiting for transfers between devices: 135 us -> 0 us
  local copies, waits for them, and re-layouts: 123 us -> 9.73 us
  other arithmetic: 38.9 us -> 0.65 us
  matrix products: 29.2 us -> 0 us
    pallas_call x0 -> x1, Pallas kernels: none -> 169 us  [per_device(): pl.pallas_call(functools.partial(relax_kernel, reach, bands), out_shape=j...]
    ppermute x10 -> x0, starting transfers between devices: 136 us -> none  [the longest x6 126 us: from_behind(): lax.ppermute(value, axis, [(source, source + steps) for source in range(f...]
    ppermute x10 -> x0, waiting for transfers between devices: 135 us -> none  [the longest x6 92.9 us: from_behind(): lax.ppermute(value, axis, [(source, source + steps) for source in range(f...]
    gather x15 -> x0, local copies, waits for them, and re-layouts: 90.2 us -> none  [the longest x4 42.9 us: one_row(): weights = jnp.take(weight_table, row_weights, axis=0)]
    dot_general x4 -> x0, matrix products: 29.2 us -> none  [one_row(): jnp.einsum('nrpy,nryx->pnx', sources, weights, preferred_element_type=jnp...]
    div x3 -> x0, other arithmetic: 26.8 us -> none  [the longest x2 23.7 us: per_device(): field = (departed + couple(field, extended[2:] + extended[:-2])) / diagonal]
    slice x6 -> x0, local copies, waits for them, and re-layouts: 12.5 us -> none  [the longest x4 12.1 us: couple(): east_west = jnp.roll(field, 1, axis=3) + jnp.roll(field, -1, axis=3)]
    unnamed x6 -> x0, other arithmetic: 8.89 us -> none
  transfers between devices with their start and end apart: 10 -> 0, of which waited for: 6 -> 0; matrix products, arithmetic and copies ran while one was open for 9% -> 0% of each run, Pallas kernels for 0% -> 0%
where the time goes in v1:
time: 180 us; the launch traced here: 179 us
  Pallas kernels  169 us (94%)
  local copies, waits for them, and re-layouts  9.73 us (5%)
    pallas_call x1, Pallas kernels, per_device(): pl.pallas_call(functools.partial(relax_kernel, reach, bands), out_shape=j...  169 us
    unnamed x5, local copies, waits for them, and re-layouts  9.73 us

profile of v1, /device:TPU:14, one launch (start us, length us, event | category | flops | bytes accessed | tf_op | source)
XLA Modules:
  0.0 179.4 jit_solution(11233192364334839777)
XLA Ops:
  0.0 1.3 copy.17
  1.3 0.8 copy.11
  2.1 0.8 copy.13
  2.9 0.7 multiply_add_fusion.pool_index_hbm
  3.5 1.4 copy.14.weight_index_hbm
  5.0 169.0 %shard_map.73 = f32[4,64,5120]{2,1,0:T(8,128)} custom-call(bf16[160,64,128]{2,1,0:T(8,128)(2,1)} %bitcast.6, s32[7,64]{1,0:T(8,128)} %bitcast.7, s32[7,64]{1,0:T(8,128)} %bitcast.8, f32[4,5120]{1,0:T(4,128)} %helm_ref.1, bf16[64,128,128]{2,1,0:T(8,128)(2,1)} %table_hbm.1, s32[4,40,8]{2,1,0:T(8,128)} %multiply_add_fusion.pool_index_hbm, ...), custom_call_target="tpu_custom_call" | custom-call | flops 2684354560 | bytes 9961472 | tf_op jit(solution)/shard_map/pallas_call | solution.py:328
  174.0 5.4 %copy.19 = f32[4,4,16,5120]{3,2,1,0:T(8,128)} copy(f32[4,4,16,5120]{3,2,1,0:T(8,128)} %bitcast.5) | data formatting | bytes 10485760

commit v2 on v1

--- a/solution.py
+++ b/solution.py
@@ -25,11 +25,13 @@
     lists_smem,
     lists_vmem,
     helm_ref,
+    owner_ref,
+    slot_ref,
     table_hbm,
-    pool_index_hbm,
     weight_index_hbm,
     out_hbm,
     table,
+    pool_vmem,
     pool_index,
     weight_index,
     asked_vmem,
@@ -40,6 +42,12 @@
     departed,
     first,
     second,
+    near_out,
+    near_in,
+    code_out,
+    code_in,
+    step_out,
+    step_in,
     local_sem,
     list_send,
     list_recv,
@@ -51,11 +59,11 @@
     out_sem,
 ):
     me = lax.axis_index("lat")
-    offsets, cap = lists_smem.shape
+    offsets, _, cap = lists_smem.shape
     rows, planes, lon = departed.shape
     width = fields_ref.shape[2]
     nblocks = lon // width
-    taps = pool_index.shape[2]
+    taps = pool_index.shape[1]
     others = [r for r in range(offsets) if r != reach]
     others.sort(key=lambda r: -abs(r - reach))
 
@@ -91,9 +99,11 @@
         def _():
             list_copy(r).start()
 
+    place = (owner_ref[...] - me + reach) * cap + slot_ref[...]
+    pool_vmem[...] = jnp.clip(place, 0, offsets * cap - 1)
     locals_ = [
         pltpu.make_async_copy(table_hbm, table, local_sem.at[0]),
-        pltpu.make_async_copy(pool_index_hbm, pool_index, local_sem.at[1]),
+        pltpu.make_async_copy(pool_vmem, pool_index, local_sem.at[1]),
         pltpu.make_async_copy(weight_index_hbm, weight_index, local_sem.at[2]),
     ]
     for copy in locals_:
@@ -129,7 +139,7 @@
 
             def pack(j, carry):
                 for u in range(unroll):
-                    packed[r, j * unroll + u] = fields_ref[asked[r, 2 * reach - r, j * unroll + u]]
+                    packed[r, j * unroll + u] = fields_ref[asked[r, 2 * reach - r, 0, j * unroll + u]]
                 return carry
 
             lax.fori_loop(0, cap // unroll, pack, 0)
@@ -137,7 +147,7 @@
 
     def pack_own(j, carry):
         for u in range(unroll):
-            pool[reach * cap + j * unroll + u] = fields_ref[lists_smem[reach, j * unroll + u]]
+            pool[reach * cap + j * unroll + u] = fields_ref[lists_smem[reach, 0, j * unroll + u]]
         return carry
 
     lax.fori_loop(0, cap // unroll, pack_own, 0)
@@ -145,15 +155,13 @@
     total_coupling = 2.0 * (lon_coupling + lat_coupling + lev_coupling)
     inverse[...] = 1.0 / (helm_ref[...] + total_coupling)
 
-    @pl.when(me == 0)
-    def _():
-        first[0] = jnp.zeros((planes, lon), jnp.float32)
-        second[0] = jnp.zeros((planes, lon), jnp.float32)
-
-    @pl.when(me == bands - 1)
-    def _():
-        first[rows + 1] = jnp.zeros((planes, lon), jnp.float32)
-        second[rows + 1] = jnp.zeros((planes, lon), jnp.float32)
+    for side, alone in ((0, me == 0), (1, me == bands - 1)):
+
+        @pl.when(alone)
+        def _():
+            near_in[side] = jnp.zeros((planes, lon), near_in.dtype)
+            code_in[side] = jnp.zeros((planes, lon), code_in.dtype)
+            step_in[side] = jnp.zeros((FLD, 1, lon), jnp.float32)
 
     for copy in locals_:
         copy.wait()
@@ -165,29 +173,42 @@
 
     north, south = me > 0, me < bands - 1
 
-    def halo_copy(sweep, way, f):
-        held = (first, second)[sweep]
+    def halo_copy(kind, way, f):
         planes_f = pl.ds(pl.multiple_of(f * LEV, LEV), LEV)
+        sent = (near_out, code_out, step_out)[kind]
+        landed = (near_in, code_in, step_in)[kind]
+        part = f if kind == 2 else planes_f
         return pltpu.make_async_remote_copy(
-            src_ref=held.at[1 if way == 0 else rows, planes_f],
-            dst_ref=held.at[rows + 1 if way == 0 else 0, planes_f],
-            send_sem=halo_send.at[sweep, way, f],
-            recv_sem=halo_recv.at[sweep, way, f],
+            src_ref=sent.at[way, part],
+            dst_ref=landed.at[1 - way, part],
+            send_sem=halo_send.at[kind, way, f],
+            recv_sem=halo_recv.at[kind, way, f],
             device_id={"lat": me - 1 if way == 0 else me + 1},
             device_id_type=MESH,
         )
 
     def interpolate(row):
-        def one_block(b, carry):
+        def one_block(b):
             columns = pl.ds(pl.multiple_of(b * width, width), width)
-            sources = jnp.concatenate([pool[pool_index[row, b, t]] for t in range(taps)], axis=1)
-            weights = jnp.concatenate([table[weight_index[row, b, t]] for t in range(taps)], axis=0)
+            sources = jnp.concatenate([pool[pool_index[row, t, b]] for t in range(taps)], axis=1)
+            weights = jnp.concatenate([table[weight_index[row, t, b]] for t in range(taps)], axis=0)
             value = jnp.dot(sources, weights, preferred_element_type=jnp.float32)
             departed[row, :, columns] = value
-            first[row + 1, :, columns] = value * inverse[row : row + 1, columns]
+            start = value * inverse[row : row + 1, columns]
+            first[row, :, columns] = start
+            if row == 0:
+                near_out[0, :, columns] = start.astype(near_out.dtype)
+            if row == rows - 1:
+                near_out[1, :, columns] = start.astype(near_out.dtype)
+
+        pair = 2 if nblocks % 2 == 0 else 1
+
+        def some_blocks(b, carry):
+            for u in range(pair):
+                one_block(b * pair + u)
             return carry
 
-        lax.fori_loop(0, nblocks, one_block, 0)
+        lax.fori_loop(0, nblocks // pair, some_blocks, 0)
 
     order = [0, rows - 1] + list(range(1, rows - 1))
     for row in order:
@@ -209,13 +230,28 @@
     chunk = 1024 if lon % 1024 == 0 else width
     lane = 128
 
+    def row_of(held, row, f, planes_f, here):
+        if 0 <= row < rows:
+            return held[row, planes_f, here]
+        side = 0 if row < 0 else 1
+        if held is first:
+            return near_in[side, planes_f, here].astype(jnp.float32)
+        codes = code_in[side, planes_f, here].astype(jnp.int32).astype(jnp.float32)
+        return codes * step_in[side, f, :, here]
+
+    def encode(value, way, f, planes_f, here):
+        largest = jnp.maximum(jnp.max(jnp.abs(value), axis=0, keepdims=True), 1e-30)
+        codes = jnp.floor(value * (32767.0 / largest) + 0.5)
+        code_out[way, planes_f, here] = codes.astype(jnp.int32).astype(jnp.int16)
+        step_out[way, f, :, here] = largest * (1.0 / 32767.0)
+
     def relax(held, result, row, f):
         planes_f = pl.ds(pl.multiple_of(f * LEV, LEV), LEV)
         for start in range(0, lon, chunk):
             here = pl.ds(start, chunk)
-            mid = held[row + 1, planes_f, here]
-            west = held[row + 1, planes_f, pl.ds((start - lane) % lon, lane)]
-            east = held[row + 1, planes_f, pl.ds((start + chunk) % lon, lane)]
+            mid = held[row, planes_f, here]
+            west = held[row, planes_f, pl.ds((start - lane) % lon, lane)]
+            east = held[row, planes_f, pl.ds((start + chunk) % lon, lane)]
             wide = jnp.concatenate([west, mid, east], axis=1)
             span = chunk + 2 * lane
             beside = pltpu.roll(wide, 1, 1) + pltpu.roll(wide, span - 1, 1)
@@ -223,13 +259,14 @@
             level = lax.broadcasted_iota(jnp.int32, (LEV, chunk), 0)
             above = jnp.where(level > 0, pltpu.roll(mid, 1, 0), 0.0)
             below = jnp.where(level < LEV - 1, pltpu.roll(mid, LEV - 1, 0), 0.0)
-            across = held[row, planes_f, here] + held[row + 2, planes_f, here]
+            across = row_of(held, row - 1, f, planes_f, here) + row_of(held, row + 1, f, planes_f, here)
             coupled = lon_coupling * beside + lat_coupling * across + lev_coupling * (above + below)
             value = (departed[row, planes_f, here] + coupled) * inverse[row : row + 1, here]
-            if result is departed:
-                result[row, planes_f, here] = value
-            else:
-                result[row + 1, planes_f, here] = value
+            result[row, planes_f, here] = value
+            if held is first and row == 0:
+                encode(value, 0, f, planes_f, here)
+            if held is first and row == rows - 1:
+                encode(value, 1, f, planes_f, here)
 
     def out_copy(row, f):
         planes_f = pl.ds(pl.multiple_of(f * LEV, LEV), LEV)
@@ -237,14 +274,18 @@
 
     inner, edges = list(range(1, rows - 1)), [0, rows - 1]
 
+    kinds = ((0,), (1, 2))
+
     def arrived(sweep, f):
         @pl.when(north)
         def _():
-            halo_copy(sweep, 1, f).wait_recv()
+            for kind in kinds[sweep]:
+                halo_copy(kind, 1, f).wait_recv()
 
         @pl.when(south)
         def _():
-            halo_copy(sweep, 0, f).wait_recv()
+            for kind in kinds[sweep]:
+                halo_copy(kind, 0, f).wait_recv()
 
     def first_inner(f, carry):
         for row in inner:
@@ -259,13 +300,15 @@
 
         @pl.when(north)
         def _():
-            halo_copy(1, 0, f).start()
+            for kind in kinds[1]:
+                halo_copy(kind, 0, f).start()
 
         relax(first, second, rows - 1, f)
 
         @pl.when(south)
         def _():
-            halo_copy(1, 1, f).start()
+            for kind in kinds[1]:
+                halo_copy(kind, 1, f).start()
 
         return carry
 
@@ -296,15 +339,15 @@
             block_copy(r).wait_send()
 
     def finish(f, carry):
-        for sweep in range(SWEEPS):
+        for kind in range(3):
 
             @pl.when(north)
             def _():
-                halo_copy(sweep, 0, f).wait_send()
+                halo_copy(kind, 0, f).wait_send()
 
             @pl.when(south)
             def _():
-                halo_copy(sweep, 1, f).wait_send()
+                halo_copy(kind, 1, f).wait_send()
 
         for row in range(rows):
             out_copy(row, f).wait()
@@ -318,9 +361,9 @@
     offsets, cap = fetch_list.shape[1:]
     reach = (offsets - 1) // 2
     lon = nblocks * width
-    position = lax.axis_index("lat")
-    lists = fetch_list[0]
-    pool_index = (source_owner - position + reach) * cap + source_slot
+    taps = source_owner.shape[2]
+    lists = fetch_list.transpose(1, 0, 2)
+    owner, slot, weight = (x.transpose(0, 2, 1) for x in (source_owner, source_slot, weight_index))
     vmem = pl.BlockSpec(memory_space=pltpu.VMEM)
     smem = pl.BlockSpec(memory_space=pltpu.SMEM)
     anywhere = pl.BlockSpec(memory_space=pl.ANY)
@@ -328,39 +371,46 @@
     result = pl.pallas_call(
         functools.partial(relax_kernel, reach, bands),
         out_shape=jax.ShapeDtypeStruct((rows, planes, lon), jnp.float32),
-        in_specs=[vmem, smem, vmem, vmem, anywhere, anywhere, anywhere],
+        in_specs=[vmem, smem, vmem, vmem, vmem, vmem, anywhere, anywhere],
         out_specs=anywhere,
         scratch_shapes=[
             pltpu.VMEM(weight_table.shape, weight_table.dtype),
-            pltpu.SMEM(pool_index.shape, jnp.int32),
-            pltpu.SMEM(weight_index.shape, jnp.int32),
-            pltpu.VMEM((offsets, offsets, cap), jnp.int32),
-            pltpu.SMEM((offsets, offsets, cap), jnp.int32),
+            pltpu.VMEM((rows, taps, nblocks), jnp.int32),
+            pltpu.SMEM((rows, taps, nblocks), jnp.int32),
+            pltpu.SMEM((rows, taps, nblocks), jnp.int32),
+            pltpu.VMEM((offsets, offsets, 1, cap), jnp.int32),
+            pltpu.SMEM((offsets, offsets, 1, cap), jnp.int32),
             pltpu.VMEM((offsets, cap, planes, width), fields.dtype),
             pltpu.VMEM((offsets * cap, planes, width), fields.dtype),
             pltpu.VMEM((rows, lon), jnp.float32),
             pltpu.VMEM((rows, planes, lon), jnp.float32),
-            pltpu.VMEM((rows + 2, planes, lon), jnp.float32),
-            pltpu.VMEM((rows + 2, planes, lon), jnp.float32),
+            pltpu.VMEM((rows, planes, lon), jnp.float32),
+            pltpu.VMEM((rows, planes, lon), jnp.float32),
+            pltpu.VMEM((2, planes, lon), jnp.bfloat16),
+            pltpu.VMEM((2, planes, lon), jnp.bfloat16),
+            pltpu.VMEM((2, planes, lon), jnp.int16),
+            pltpu.VMEM((2, planes, lon), jnp.int16),
+            pltpu.VMEM((2, FLD, 1, lon), jnp.float32),
+            pltpu.VMEM((2, FLD, 1, lon), jnp.float32),
             dma((3,)),
             dma((offsets,)),
             dma((offsets,)),
             dma((offsets,)),
             dma((offsets,)),
             dma((offsets,)),
-            dma((SWEEPS, 2, FLD)),
-            dma((SWEEPS, 2, FLD)),
+            dma((3, 2, FLD)),
+            dma((3, 2, FLD)),
             dma((rows, FLD)),
         ],
         compiler_params=pltpu.CompilerParams(
-            collective_id=0, has_side_effects=True, vmem_limit_bytes=56 * 1024 * 1024
+            collective_id=0, has_side_effects=True, vmem_limit_bytes=46 * 1024 * 1024
         ),
         cost_estimate=pl.CostEstimate(
             flops=2 * source_owner.size * planes * width * width,
             bytes_accessed=fields.size * 2 + weight_table.size * 2 + rows * planes * lon * 4,
             transcendentals=0,
         ),
-    )(fields.reshape(rows * nblocks, planes, width), lists, lists, helm_coef, weight_table, pool_index, weight_index)
+    )(fields.reshape(rows * nblocks, planes, width), lists, lists, helm_coef, owner, slot, weight_table, weight)
     return result.reshape(rows, FLD, LEV, lon)
 
 

time: 180 us -> 152 us (0.84)
  Pallas kernels: 169 us -> 139 us
  local copies, waits for them, and re-layouts: 9.73 us -> 12.5 us
    pallas_call x1, Pallas kernels: 169 us -> 139 us  [per_device(): pl.pallas_call(functools.partial(relax_kernel, reach, bands), out_shape=j...]
    unnamed x5 -> x15, local copies, waits for them, and re-layouts: 9.73 us -> 12.5 us
where the time goes in v2:
time: 152 us; the launch traced here: 151 us
  Pallas kernels  139 us (91%)
  local copies, waits for them, and re-layouts  12.5 us (8%)
    pallas_call x1, Pallas kernels, per_device(): pl.pallas_call(functools.partial(relax_kernel, reach, bands), out_shape=j...  139 us
    unnamed x15, local copies, waits for them, and re-layouts  12.5 us

profile of v2, /device:TPU:14, one launch (start us, length us, event | category | flops | bytes accessed | tf_op | source)
XLA Modules:
  0.0 151.2 jit_solution(4785678832001833987)
XLA Ops:
  0.0 0.0 copy-start
  0.0 1.7 %copy-done = bf16[4,40,64,128]{3,2,1,0:T(8,128)(2,1)S(1)} copy-done((bf16[4,40,64,128]{3,2,1,0:T(8,128)(2,1)S(1)}, bf16[4,40,64,128]{3,2,1,0:T(8,128)(2,1)}, u32[]{:S(2)}) %copy-start) | copy-done | bytes 2621464
  1.7 0.0 copy-start.1
  1.7 1.6 %copy-done.1 = bf16[64,128,128]{2,1,0:T(8,128)(2,1)S(1)} copy-done((bf16[64,128,128]{2,1,0:T(8,128)(2,1)S(1)}, bf16[64,128,128]{2,1,0:T(8,128)(2,1)}, u32[]{:S(2)}) %copy-start.1) | copy-done | bytes 2097176
  3.3 0.0 copy-start.2
  3.3 0.9 copy-done.2
  4.2 0.0 copy-start.3
  4.2 0.7 copy-done.3
  4.9 0.0 copy-start.4
  4.9 0.7 copy-done.4
  5.7 0.0 copy-start.5
  5.7 0.7 copy-done.5
  6.4 0.0 copy-start.6
  6.4 0.7 copy-done.6
  7.1 138.7 %shard_map.73 = f32[4,64,5120]{2,1,0:T(8,128)} custom-call(bf16[160,64,128]{2,1,0:T(8,128)(2,1)S(1)} %bitcast.6, s32[7,1,64]{2,1,0:T(1,128)S(1)} %bitcast.10, s32[7,1,64]{2,1,0:T(1,128)S(1)} %bitcast.11, f32[4,5120]{1,0:T(4,128)S(1)} %copy-done.2, s32[4,8,40]{2,1,0:T(8,128)S(1)} %bitcast.7, s32[4,8,40]{2,1,0:T(8,128)S(1)} %bitcast.8, ...), custom_call_target="tpu_custom_call" | custom-call | flops 2684354560 | bytes 9961472 | tf_op jit(solution)/shard_map/pallas_call | solution.py:371
  145.8 5.4 %copy.9 = f32[4,4,16,5120]{3,2,1,0:T(8,128)} copy(f32[4,4,16,5120]{3,2,1,0:T(8,128)} %bitcast.12) | data formatting | bytes 10485760
Async XLA Ops:
  0.0 1.7 %copy-start = (bf16[4,40,64,128]{3,2,1,0:T(8,128)(2,1)S(1)}, bf16[4,40,64,128]{3,2,1,0:T(8,128)(2,1)}, u32[]{:S(2)}) copy-start(bf16[4,40,64,128]{3,2,1,0:T(8,128)(2,1)} %param.7) | copy-start | bytes 7864324
  1.7 1.6 %copy-start.1 = (bf16[64,128,128]{2,1,0:T(8,128)(2,1)S(1)}, bf16[64,128,128]{2,1,0:T(8,128)(2,1)}, u32[]{:S(2)}) copy-start(bf16[64,128,128]{2,1,0:T(8,128)(2,1)} %table_hbm.1) | copy-start | bytes 6291460
  3.3 0.9 copy-start.2
  4.2 0.7 copy-start.3
  4.9 0.7 copy-start.4
  5.7 0.7 copy-start.5
  6.4 0.7 copy-start.6

commit v3 on v2

--- a/solution.py
+++ b/solution.py
@@ -21,15 +21,18 @@
 def relax_kernel(
     reach,
     bands,
-    fields_ref,
-    lists_smem,
-    lists_vmem,
-    helm_ref,
-    owner_ref,
-    slot_ref,
+    fields_hbm,
+    lists_hbm,
+    helm_hbm,
+    owner_hbm,
+    slot_hbm,
     table_hbm,
     weight_index_hbm,
     out_hbm,
+    fields_ref,
+    lists_smem,
+    owner_ref,
+    slot_ref,
     table,
     pool_vmem,
     pool_index,
@@ -71,6 +74,19 @@
         band = me + (step - reach)
         return (band >= 0) & (band < bands)
 
+    brought = (
+        (fields_hbm, fields_ref),
+        (owner_hbm, owner_ref),
+        (slot_hbm, slot_ref),
+        (lists_hbm, lists_smem),
+        (weight_index_hbm, weight_index),
+        (helm_hbm, inverse),
+        (table_hbm, table),
+    )
+    locals_ = [pltpu.make_async_copy(a, b, local_sem.at[k]) for k, (a, b) in enumerate(brought)]
+    for copy in locals_:
+        copy.start()
+
     barrier = pltpu.get_barrier_semaphore()
     count = jnp.int32(0)
     for r in others:
@@ -85,7 +101,7 @@
     def list_copy(r):
         back = 2 * reach - r
         return pltpu.make_async_remote_copy(
-            src_ref=lists_vmem,
+            src_ref=lists_hbm,
             dst_ref=asked_vmem.at[back],
             send_sem=list_send.at[r],
             recv_sem=list_recv.at[back],
@@ -99,15 +115,12 @@
         def _():
             list_copy(r).start()
 
+    locals_[1].wait()
+    locals_[2].wait()
     place = (owner_ref[...] - me + reach) * cap + slot_ref[...]
     pool_vmem[...] = jnp.clip(place, 0, offsets * cap - 1)
-    locals_ = [
-        pltpu.make_async_copy(table_hbm, table, local_sem.at[0]),
-        pltpu.make_async_copy(pool_vmem, pool_index, local_sem.at[1]),
-        pltpu.make_async_copy(weight_index_hbm, weight_index, local_sem.at[2]),
-    ]
-    for copy in locals_:
-        copy.start()
+    pool_copy = pltpu.make_async_copy(pool_vmem, pool_index, local_sem.at[len(brought)])
+    pool_copy.start()
 
     def asked_copy(r):
         return pltpu.make_async_copy(asked_vmem.at[r], asked.at[r], asked_sem.at[r])
@@ -118,6 +131,8 @@
         def _():
             list_copy(2 * reach - r).wait_recv()
             asked_copy(r).start()
+
+    locals_[0].wait()
 
     def block_copy(r):
         back = 2 * reach - r
@@ -145,6 +160,10 @@
             lax.fori_loop(0, cap // unroll, pack, 0)
             block_copy(r).start()
 
+    for copy in locals_[3:]:
+        copy.wait()
+    pool_copy.wait()
+
     def pack_own(j, carry):
         for u in range(unroll):
             pool[reach * cap + j * unroll + u] = fields_ref[lists_smem[reach, 0, j * unroll + u]]
@@ -153,7 +172,7 @@
     lax.fori_loop(0, cap // unroll, pack_own, 0)
 
     total_coupling = 2.0 * (lon_coupling + lat_coupling + lev_coupling)
-    inverse[...] = 1.0 / (helm_ref[...] + total_coupling)
+    inverse[...] = 1.0 / (inverse[...] + total_coupling)
 
     for side, alone in ((0, me == 0), (1, me == bands - 1)):
 
@@ -163,8 +182,6 @@
             code_in[side] = jnp.zeros((planes, lon), code_in.dtype)
             step_in[side] = jnp.zeros((FLD, 1, lon), jnp.float32)
 
-    for copy in locals_:
-        copy.wait()
     for r in others:
 
         @pl.when(there(r))
@@ -287,13 +304,6 @@
             for kind in kinds[sweep]:
                 halo_copy(kind, 0, f).wait_recv()
 
-    def first_inner(f, carry):
-        for row in inner:
-            relax(first, second, row, f)
-        return carry
-
-    lax.fori_loop(0, FLD, first_inner, 0)
-
     def first_edges(f, carry):
         arrived(0, f)
         relax(first, second, 0, f)
@@ -310,6 +320,8 @@
             for kind in kinds[1]:
                 halo_copy(kind, 1, f).start()
 
+        for row in inner:
+            relax(first, second, row, f)
         return carry
 
     lax.fori_loop(0, FLD, first_edges, 0)
@@ -364,16 +376,18 @@
     taps = source_owner.shape[2]
     lists = fetch_list.transpose(1, 0, 2)
     owner, slot, weight = (x.transpose(0, 2, 1) for x in (source_owner, source_slot, weight_index))
-    vmem = pl.BlockSpec(memory_space=pltpu.VMEM)
-    smem = pl.BlockSpec(memory_space=pltpu.SMEM)
     anywhere = pl.BlockSpec(memory_space=pl.ANY)
     dma = pltpu.SemaphoreType.DMA
     result = pl.pallas_call(
         functools.partial(relax_kernel, reach, bands),
         out_shape=jax.ShapeDtypeStruct((rows, planes, lon), jnp.float32),
-        in_specs=[vmem, smem, vmem, vmem, vmem, vmem, anywhere, anywhere],
+        in_specs=[anywhere] * 7,
         out_specs=anywhere,
         scratch_shapes=[
+            pltpu.VMEM((rows * nblocks, planes, width), fields.dtype),
+            pltpu.SMEM((offsets, 1, cap), jnp.int32),
+            pltpu.VMEM((rows, taps, nblocks), jnp.int32),
+            pltpu.VMEM((rows, taps, nblocks), jnp.int32),
             pltpu.VMEM(weight_table.shape, weight_table.dtype),
             pltpu.VMEM((rows, taps, nblocks), jnp.int32),
             pltpu.SMEM((rows, taps, nblocks), jnp.int32),
@@ -392,7 +406,7 @@
             pltpu.VMEM((2, planes, lon), jnp.int16),
             pltpu.VMEM((2, FLD, 1, lon), jnp.float32),
             pltpu.VMEM((2, FLD, 1, lon), jnp.float32),
-            dma((3,)),
+            dma((8,)),
             dma((offsets,)),
             dma((offsets,)),
             dma((offsets,)),
@@ -403,14 +417,14 @@
             dma((rows, FLD)),
         ],
         compiler_params=pltpu.CompilerParams(
-            collective_id=0, has_side_effects=True, vmem_limit_bytes=46 * 1024 * 1024
+            collective_id=0, has_side_effects=True, vmem_limit_bytes=58 * 1024 * 1024
         ),
         cost_estimate=pl.CostEstimate(
             flops=2 * source_owner.size * planes * width * width,
             bytes_accessed=fields.size * 2 + weight_table.size * 2 + rows * planes * lon * 4,
             transcendentals=0,
         ),
-    )(fields.reshape(rows * nblocks, planes, width), lists, lists, helm_coef, owner, slot, weight_table, weight)
+    )(fields.reshape(rows * nblocks, planes, width), lists, helm_coef, owner, slot, weight_table, weight)
     return result.reshape(rows, FLD, LEV, lon)
 
 

time: 152 us -> 144 us (0.947)
  local copies, waits for them, and re-layouts: 12.5 us -> 5.41 us
    unnamed x15 -> x1, local copies, waits for them, and re-layouts: 12.5 us -> 5.41 us
where the time goes in v3:
time: 144 us
  Pallas kernels  138 us (96%)
  local copies, waits for them, and re-layouts  5.41 us (4%)
    pallas_call x1, Pallas kernels, per_device(): pl.pallas_call(functools.partial(relax_kernel, reach, bands), out_shape=j...  138 us
    unnamed x1, local copies, waits for them, and re-layouts  5.41 us

profile of v3, /device:TPU:14, one launch (start us, length us, event | category | flops | bytes accessed | tf_op | source)
XLA Modules:
  0.0 143.8 jit_solution(9409216849120895933)
XLA Ops:
  0.0 138.4 %shard_map.73 = f32[4,64,5120]{2,1,0:T(8,128)} custom-call(bf16[160,64,128]{2,1,0:T(8,128)(2,1)} %bitcast.7, s32[7,1,64]{2,1,0:T(1,128)} %bitcast.11, f32[4,5120]{1,0:T(4,128)} %helm_hbm.1, s32[4,8,40]{2,1,0:T(8,128)} %bitcast.8, s32[4,8,40]{2,1,0:T(8,128)} %bitcast.9, bf16[64,128,128]{2,1,0:T(8,128)(2,1)} %table_hbm.1, s32[4,8,40]{2,1,0:T(8,128)} %bitcast.10), custom_call_target="tpu_custom_call" | custom-call | flops 2684354560 | bytes 9961472 | tf_op jit(solution)/shard_map/pallas_call | solution.py:381
  138.4 5.4 %copy.9 = f32[4,4,16,5120]{3,2,1,0:T(8,128)} copy(f32[4,4,16,5120]{3,2,1,0:T(8,128)} %bitcast.6) | data formatting | bytes 10485760
